TPU v7x, 32 devices: a whole 2x2x4 slice. The times are simulated.
32 devices in a mesh: region: 8 (over y, x, core), shard: 4 (over z).
Axes of the slice: x: 2, y: 2, z: 4, core: 2. Of those that a mesh axis runs over, the one named last changes fastest.
Arguments:
- state_anom: float32 [32768, 256], P(('region', 'shard')), may hold values from -6 to 6
- state_mean: float32 [32768], P(('region', 'shard')), may hold values from -6 to 6
- obs_anom: float32 [16, 512, 256], P('region', 'shard'), may hold values from -6 to 6
- obs_depart: float32 [16, 512], P('region', 'shard'), may hold values from -6 to 6
- obs_var: float32 [16, 512], P('region', 'shard'), may hold values from 0.5 to 2
- taper_levels: float32 [8], replicated, may hold values from 0 to 1
- state_taper: int32 [256, 64], P(('region', 'shard')), may hold values from 0 to 7
- obs_taper: int32 [64, 64], P('region'), may hold values from 0 to 7
- batch_order: int32 [3], replicated, may hold values from 0 to 15, as said below
Outputs:
- post_anom: float32 [32768, 256], P(('region', 'shard'))
- post_mean: float32 [32768], P(('region', 'shard'))
- post_obs_anom: float32 [16, 512, 256], P('region', 'shard')
- post_obs_depart: float32 [16, 512], P('region', 'shard')
Inputs may be any that keep to these rules, and one draw needn't show every extreme that they name: `batch_order`: 3 distinct batch numbers; batch q lies in region q // 2; the first and the last batch number both occur.
All inputs are finite; a program needn't handle non-finite values.
Results may differ from a plain program's by a relative error of at most 0.0001.
Values sent between devices are 32-bit elements; how exact they have to be, the bound alone decides.
A program may use at most 64 MiB of HBM per device.

v0:
```python
import jax
import jax.numpy as jnp
from jax import lax
from jax.sharding import PartitionSpec as P

M = 256
P_SIZE = 512
TAPER_BLOCK = 128
NB = 3
KB = 2


highest = lax.Precision.HIGHEST


def from_root(block, axis, source):
    block = jnp.where(lax.axis_index(axis) == source, block, jnp.zeros_like(block))
    return lax.psum(block, axis)


def factorize(anomalies, departs, variances):
    product = jnp.dot(anomalies, anomalies.T, precision=highest, preferred_element_type=jnp.float32)
    system = product / (M - 1) + jnp.diag(variances)
    lower_factor = jnp.linalg.cholesky(system)
    shifted = lower_factor + jnp.diag(jnp.sqrt(variances))
    solved = lax.linalg.triangular_solve(shifted, anomalies, left_side=True, lower=True)
    increments = lax.linalg.triangular_solve(
        lower_factor, solved, left_side=True, lower=True, transpose_a=True
    )
    first = lax.linalg.triangular_solve(lower_factor, departs[:, None], left_side=True, lower=True)
    weights = lax.linalg.triangular_solve(
        lower_factor, first, left_side=True, lower=True, transpose_a=True
    )
    return (increments, weights[:, 0])


def lookup(levels, index):
    levels_count = levels.shape[0]
    onehot = (index[..., None] == jnp.arange(levels_count, dtype=jnp.int32)).astype(jnp.float32)
    return jnp.sum(onehot * levels, axis=-1)


def covariance(rows, batch_rows):
    product = lax.dot_general(
        rows,
        batch_rows,
        (((1,), (1,)), ((), ())),
        precision=highest,
        preferred_element_type=jnp.float32,
    )
    return product / (M - 1)


def apply_rows(covar, increments, weights):
    delta_rows = jnp.dot(covar, increments, precision=highest, preferred_element_type=jnp.float32)
    delta_mean = jnp.dot(covar, weights, precision=highest, preferred_element_type=jnp.float32)
    return (delta_rows, delta_mean)


def per_device(
    state_anom,
    state_mean,
    obs_anom,
    obs_depart,
    obs_var,
    taper_levels,
    state_taper,
    obs_taper,
    batch_order,
):
    shard_pos = lax.axis_index("shard")
    pieces = obs_anom.shape[1]
    blocks = P_SIZE // TAPER_BLOCK
    obs_rows = obs_anom.shape[0] * pieces
    state_rows = state_anom.shape[0]
    row_block = (
        jnp.arange(KB, dtype=jnp.int32)[:, None] * P_SIZE
        + shard_pos * pieces
        + jnp.arange(pieces, dtype=jnp.int32)[None, :]
    ).reshape(obs_rows) // TAPER_BLOCK
    anomaly = state_anom
    mean_state = state_mean
    obs_now = obs_anom.reshape(obs_rows, M)
    depart_now = obs_depart.reshape(obs_rows)
    for section_idx in range(NB):
        batch_id = batch_order[section_idx]
        owner_id = batch_id // KB
        local_id = batch_id % KB
        rows_piece = lax.dynamic_slice_in_dim(obs_now, local_id * pieces, pieces, 0)
        depart_piece = lax.dynamic_slice_in_dim(depart_now, local_id * pieces, pieces, 0)
        var_piece = lax.dynamic_index_in_dim(obs_var, local_id, 0, keepdims=False)
        sent_rows, sent_depart, sent_var = (
            from_root(rows_piece, "region", owner_id),
            from_root(depart_piece, "region", owner_id),
            from_root(var_piece, "region", owner_id),
        )
        batch_rows, departs, variances = (
            lax.all_gather(sent_rows, "shard", axis=0, tiled=True),
            lax.all_gather(sent_depart, "shard", axis=0, tiled=True),
            lax.all_gather(sent_var, "shard", axis=0, tiled=True),
        )
        increments, weights = factorize(batch_rows, departs, variances)
        state_cols = lax.dynamic_slice_in_dim(state_taper, batch_id * blocks, blocks, 1)
        state_weights = lookup(taper_levels, state_cols)
        covar = covariance(anomaly, batch_rows)
        covar = (
            covar.reshape(state_rows // TAPER_BLOCK, TAPER_BLOCK, blocks, TAPER_BLOCK)
            * state_weights[:, None, :, None]
        )
        covar = covar.reshape(state_rows, P_SIZE)
        delta_rows, delta_mean = apply_rows(covar, increments, weights)
        obs_cols = lax.dynamic_slice_in_dim(obs_taper, batch_id * blocks, blocks, 1)
        obs_weights = lookup(taper_levels, jnp.take(obs_cols, row_block, axis=0))
        covar_obs = (
            covariance(obs_now, batch_rows).reshape(obs_rows, blocks, TAPER_BLOCK)
            * obs_weights[:, :, None]
        )
        covar_obs = covar_obs.reshape(obs_rows, P_SIZE)
        delta_obs, delta_depart = apply_rows(covar_obs, increments, weights)
        anomaly = anomaly - delta_rows
        mean_state = mean_state + delta_mean
        obs_now = obs_now - delta_obs
        depart_now = depart_now - delta_depart
    return (
        anomaly,
        mean_state,
        obs_now.reshape(obs_anom.shape),
        depart_now.reshape(obs_depart.shape),
    )


def solution(mesh):
    placed = (
        P(("region", "shard"), None),
        P(("region", "shard")),
        P("region", "shard", None),
        P("region", "shard"),
        P("region", "shard"),
        P(),
        P(("region", "shard"), None),
        P("region", None),
        P(),
    )
    return jax.shard_map(
        per_device,
        mesh=mesh,
        in_specs=placed,
        out_specs=(
            P(("region", "shard"), None),
            P(("region", "shard")),
            P("region", "shard", None),
            P("region", "shard"),
        ),
        check_vma=False,
    )
```

profile of v0, /device:TPU:0, one launch (start us, length us, event | category | flops | bytes accessed | tf_op | source)
XLA Modules:
  0.0 909.8 jit_solution(10384366088618629385)
XLA Ops:
  22.2 15.1 %all-reduce.3 = (f32[128]{0:T(128)S(1)}, f32[128]{0:T(128)S(1)}) all-reduce(f32[128]{0:T(128)S(1)} %get-tuple-element.351, f32[128]{0:T(128)S(1)} %broadcast_select_fusion.5), channel_id=1, replica_groups=mesh['region'=8,'shard'=4] {'region'}, use_global_device_ids=true, to_apply=%region_2.3 | all-reduce | flops 256 | bytes 2048 | tf_op jit(solution)/shard_map/psum | solution.py:18
  37.3 11.1 %all-gather = f32[4,1,128]{2,1,0:T(1,128)S(1)} all-gather(f32[1,1,128]{2,1,0:T(1,128)S(1)} %bitcast.655), channel_id=1, replica_groups=mesh['region'=8,'shard'=4] {'shard'}, dimensions={0}, use_global_device_ids=true | all-gather | bytes 2560 | tf_op jit(solution)/shard_map/all_gather | solution.py:100
  52.9 7.5 all-gather.3
  61.7 6.9 all-reduce.8.cloned.1.call-done
  68.6 15.2 %all_gather.27 = f32[512,256]{1,0:T(8,128)S(1)} all-gather(f32[128,256]{1,0:T(8,128)} %all-reduce.8.cloned.1.call-done), channel_id=1, replica_groups=mesh['region'=8,'shard'=4] {'shard'}, dimensions={0}, use_global_device_ids=true | all-gather | bytes 655360 | tf_op jit(solution)/shard_map/all_gather | solution.py:98
  86.4 11.7 %cholesky.374 = f32[128,128]{1,0:T(8,128)S(1)} custom-call(f32[128,128]{1,0:T(8,128)S(1)} %cholesky.586), custom_call_target="Cholesky" | custom-call | tf_op jit(solution)/shard_map/jit(cholesky)/cholesky | solution.py:24
  98.2 9.8 %custom-call.46 = f32[1,128,128]{1,2,0:T(8,128)S(1)} custom-call(f32[1,128,128]{2,1,0:T(8,128)S(1)} %get-tuple-element.343), custom_call_target="InvertDiagBlocksLowerTriangular" | custom-call | tf_op jit(solution)/shard_map/jit(cholesky)/cholesky | solution.py:24
  110.5 11.7 %cholesky.393 = f32[128,128]{1,0:T(8,128)S(1)} custom-call(f32[128,128]{1,0:T(8,128)S(1)} %cholesky.590), custom_call_target="Cholesky" | custom-call | tf_op jit(solution)/shard_map/jit(cholesky)/cholesky | solution.py:24
  122.8 9.8 %custom-call.47 = f32[1,128,128]{1,2,0:T(8,128)S(1)} custom-call(f32[1,128,128]{2,1,0:T(8,128)S(1)} %get-tuple-element.341), custom_call_target="InvertDiagBlocksLowerTriangular" | custom-call | tf_op jit(solution)/shard_map/jit(cholesky)/cholesky | solution.py:24
  134.6 11.7 %cholesky.414 = f32[128,128]{1,0:T(8,128)S(1)} custom-call(f32[128,128]{1,0:T(8,128)S(1)} %cholesky.595), custom_call_target="Cholesky" | custom-call | tf_op jit(solution)/shard_map/jit(cholesky)/cholesky | solution.py:24
  146.5 9.8 %custom-call.48 = f32[1,128,128]{1,2,0:T(8,128)S(1)} custom-call(f32[1,128,128]{2,1,0:T(8,128)S(1)} %get-tuple-element.339), custom_call_target="InvertDiagBlocksLowerTriangular" | custom-call | tf_op jit(solution)/shard_map/jit(cholesky)/cholesky | solution.py:24
  157.9 12.1 %cholesky.431 = f32[128,128]{1,0:T(8,128)S(1)} custom-call(f32[128,128]{1,0:T(8,128)S(1)} %convolution_subtract_fusion.32), custom_call_target="Cholesky" | custom-call | tf_op jit(solution)/shard_map/jit(cholesky)/cholesky | solution.py:24
  175.9 12.0 %while.24 = (s32[]{:T(128)}, f32[512,512]{0,1:T(8,128)}, s32[4,2]{0,1:T(2,128)S(1)}, f32[4,128,128]{2,1,0:T(8,128)S(1)}, s32[]{:T(128)}) while((s32[]{:T(128)}, f32[512,512]{0,1:T(8,128)}, s32[4,2]{0,1:T(2,128)S(1)}, f32[4,128,128]{2,1,0:T(8,128)S(1)}, s32[]{:T(128)}) %tuple.188), condition=%wide.while_cond, body=%wide.while_body.sunk | while | flops 2 | bytes 393321 | solution.py:26
  187.9 39.3 %custom-call.49 = f32[4,128,128]{1,2,0:T(8,128)S(1)} custom-call(f32[4,128,128]{2,1,0:T(8,128)S(1)} %get-tuple-element.90), custom_call_target="InvertDiagBlocksLowerTriangular" | custom-call | tf_op jit(solution)/shard_map/triangular_solve/custom-call.3 | solution.py:26
  232.5 8.5 while.25
  240.9 39.5 %custom-call.50 = f32[4,128,128]{1,2,0:T(8,128)S(1)} custom-call(f32[4,128,128]{2,1,0:T(8,128)S(1)} %get-tuple-element.91), custom_call_target="InvertDiagBlocksLowerTriangular" | custom-call | tf_op jit(solution)/shard_map/triangular_solve/custom-call.8 | solution.py:27
  295.7 11.8 %all-reduce.2 = (f32[128]{0:T(128)S(1)}, f32[128]{0:T(128)S(1)}) all-reduce(f32[128]{0:T(128)S(1)} %get-tuple-element.352, f32[128]{0:T(128)S(1)} %broadcast_select_fusion.4), channel_id=1, replica_groups=mesh['region'=8,'shard'=4] {'region'}, use_global_device_ids=true, to_apply=%region_14.19 | all-reduce | flops 256 | bytes 2048 | tf_op jit(solution)/shard_map/psum | solution.py:18
  307.5 11.6 %all-gather.1 = f32[4,1,128]{2,1,0:T(1,128)S(1)} all-gather(f32[1,1,128]{2,1,0:T(1,128)S(1)} %bitcast.656), channel_id=1, replica_groups=mesh['region'=8,'shard'=4] {'shard'}, dimensions={0}, use_global_device_ids=true | all-gather | bytes 2560 | tf_op jit(solution)/shard_map/all_gather | solution.py:100
  319.7 7.6 all-gather.4
  327.3 21.5 %all-reduce.10.cloned.1.call-done = f32[128,256]{1,0:T(8,128)} async-done(((f32[128,256]{1,0:T(8,128)}), f32[128,256]{1,0:T(8,128)}) %all-reduce.10.cloned.1.call-update) | async-done | bytes 131088 | tf_op jit(solution)/shard_map/psum | solution.py:18
  348.8 15.4 %all_gather.29 = f32[512,256]{1,0:T(8,128)S(1)} all-gather(f32[128,256]{1,0:T(8,128)} %all-reduce.10.cloned.1.call-done), channel_id=1, replica_groups=mesh['region'=8,'shard'=4] {'shard'}, dimensions={0}, use_global_device_ids=true | all-gather | bytes 655360 | tf_op jit(solution)/shard_map/all_gather | solution.py:98
  369.0 11.7 %cholesky.446 = f32[128,128]{1,0:T(8,128)S(1)} custom-call(f32[128,128]{1,0:T(8,128)S(1)} %cholesky.599), custom_call_target="Cholesky" | custom-call | tf_op jit(solution)/shard_map/jit(cholesky)/cholesky | solution.py:24
  381.4 9.8 %custom-call.51 = f32[1,128,128]{1,2,0:T(8,128)S(1)} custom-call(f32[1,128,128]{2,1,0:T(8,128)S(1)} %get-tuple-element.337), custom_call_target="InvertDiagBlocksLowerTriangular" | custom-call | tf_op jit(solution)/shard_map/jit(cholesky)/cholesky | solution.py:24
  393.7 11.7 %cholesky.465 = f32[128,128]{1,0:T(8,128)S(1)} custom-call(f32[128,128]{1,0:T(8,128)S(1)} %cholesky.603), custom_call_target="Cholesky" | custom-call | tf_op jit(solution)/shard_map/jit(cholesky)/cholesky | solution.py:24
  407.3 9.8 %custom-call.52 = f32[1,128,128]{1,2,0:T(8,128)S(1)} custom-call(f32[1,128,128]{2,1,0:T(8,128)S(1)} %get-tuple-element.335), custom_call_target="InvertDiagBlocksLowerTriangular" | custom-call | tf_op jit(solution)/shard_map/jit(cholesky)/cholesky | solution.py:24
  420.9 11.7 %cholesky.486 = f32[128,128]{1,0:T(8,128)S(1)} custom-call(f32[128,128]{1,0:T(8,128)S(1)} %cholesky.608), custom_call_target="Cholesky" | custom-call | tf_op jit(solution)/shard_map/jit(cholesky)/cholesky | solution.py:24
  433.3 9.8 %custom-call.53 = f32[1,128,128]{1,2,0:T(8,128)S(1)} custom-call(f32[1,128,128]{2,1,0:T(8,128)S(1)} %get-tuple-element.333), custom_call_target="InvertDiagBlocksLowerTriangular" | custom-call | tf_op jit(solution)/shard_map/jit(cholesky)/cholesky | solution.py:24
  444.7 11.9 %cholesky.503 = f32[128,128]{1,0:T(8,128)S(1)} custom-call(f32[128,128]{1,0:T(8,128)S(1)} %convolution_subtract_fusion.31), custom_call_target="Cholesky" | custom-call | tf_op jit(solution)/shard_map/jit(cholesky)/cholesky | solution.py:24
  467.2 12.0 %while.26 = (s32[]{:T(128)}, f32[512,512]{0,1:T(8,128)}, s32[4,2]{0,1:T(2,128)S(1)}, f32[4,128,128]{2,1,0:T(8,128)S(1)}, s32[]{:T(128)}) while((s32[]{:T(128)}, f32[512,512]{0,1:T(8,128)}, s32[4,2]{0,1:T(2,128)S(1)}, f32[4,128,128]{2,1,0:T(8,128)S(1)}, s32[]{:T(128)}) %tuple.214), condition=%wide.while_cond.clone, body=%wide.while_body.clone.sunk | while | flops 2 | bytes 393321 | solution.py:26
  479.2 39.9 %custom-call.54 = f32[4,128,128]{1,2,0:T(8,128)} custom-call(f32[4,128,128]{2,1,0:T(8,128)S(1)} %get-tuple-element.92), custom_call_target="InvertDiagBlocksLowerTriangular" | custom-call | tf_op jit(solution)/shard_map/triangular_solve/custom-call.3 | solution.py:26
  529.1 11.0 %while.27 = (s32[]{:T(128)}, f32[512,512]{0,1:T(8,128)S(1)}, s32[4,2]{0,1:T(2,128)S(1)}, f32[4,128,128]{2,1,0:T(8,128)}, s32[]{:T(128)}) while((s32[]{:T(128)}, f32[512,512]{0,1:T(8,128)S(1)}, s32[4,2]{0,1:T(2,128)S(1)}, f32[4,128,128]{2,1,0:T(8,128)}, s32[]{:T(128)}) %tuple.215), condition=%wide.while_cond.1.clone, body=%wide.while_body.1.clone.sunk | while | flops 2 | bytes 393829 | solution.py:27
  540.1 40.9 %custom-call.55 = f32[4,128,128]{1,2,0:T(8,128)} custom-call(f32[4,128,128]{2,1,0:T(8,128)} %get-tuple-element.93), custom_call_target="InvertDiagBlocksLowerTriangular" | custom-call | tf_op jit(solution)/shard_map/triangular_solve/custom-call.8 | solution.py:27
  600.3 11.8 %all-reduce.1 = (f32[128]{0:T(128)S(1)}, f32[128]{0:T(128)S(1)}) all-reduce(f32[128]{0:T(128)S(1)} %copy-done.28, f32[128]{0:T(128)S(1)} %broadcast_select_fusion.3), channel_id=1, replica_groups=mesh['region'=8,'shard'=4] {'region'}, use_global_device_ids=true, to_apply=%region_18.23 | all-reduce | flops 256 | bytes 2048 | tf_op jit(solution)/shard_map/psum | solution.py:18
  612.0 11.6 %all-gather.2 = f32[4,1,128]{2,1,0:T(1,128)S(1)} all-gather(f32[1,1,128]{2,1,0:T(1,128)S(1)} %bitcast.657), channel_id=1, replica_groups=mesh['region'=8,'shard'=4] {'shard'}, dimensions={0}, use_global_device_ids=true | all-gather | bytes 2560 | tf_op jit(solution)/shard_map/all_gather | solution.py:100
  624.3 7.8 all-gather.5
  632.0 21.4 %all-reduce.12.cloned.1.call-done = f32[128,256]{1,0:T(8,128)} async-done(((f32[128,256]{1,0:T(8,128)}), f32[128,256]{1,0:T(8,128)}) %all-reduce.12.cloned.1.call-update) | async-done | bytes 131088 | tf_op jit(solution)/shard_map/psum | solution.py:18
  653.4 15.6 %all_gather.31 = f32[512,256]{1,0:T(8,128)S(1)} all-gather(f32[128,256]{1,0:T(8,128)} %all-reduce.12.cloned.1.call-done), channel_id=1, replica_groups=mesh['region'=8,'shard'=4] {'shard'}, dimensions={0}, use_global_device_ids=true | all-gather | bytes 655360 | tf_op jit(solution)/shard_map/all_gather | solution.py:98
  673.8 11.7 %cholesky.518 = f32[128,128]{1,0:T(8,128)S(1)} custom-call(f32[128,128]{1,0:T(8,128)S(1)} %cholesky.612), custom_call_target="Cholesky" | custom-call | tf_op jit(solution)/shard_map/jit(cholesky)/cholesky | solution.py:24
  686.1 9.8 %custom-call.56 = f32[1,128,128]{1,2,0:T(8,128)S(1)} custom-call(f32[1,128,128]{2,1,0:T(8,128)S(1)} %get-tuple-element.331), custom_call_target="InvertDiagBlocksLowerTriangular" | custom-call | tf_op jit(solution)/shard_map/jit(cholesky)/cholesky | solution.py:24
  698.4 11.7 %cholesky.537 = f32[128,128]{1,0:T(8,128)S(1)} custom-call(f32[128,128]{1,0:T(8,128)S(1)} %cholesky.616), custom_call_target="Cholesky" | custom-call | tf_op jit(solution)/shard_map/jit(cholesky)/cholesky | solution.py:24
  711.9 9.8 %custom-call.57 = f32[1,128,128]{1,2,0:T(8,128)S(1)} custom-call(f32[1,128,128]{2,1,0:T(8,128)S(1)} %get-tuple-element.329), custom_call_target="InvertDiagBlocksLowerTriangular" | custom-call | tf_op jit(solution)/shard_map/jit(cholesky)/cholesky | solution.py:24
  725.4 11.7 %cholesky.558 = f32[128,128]{1,0:T(8,128)S(1)} custom-call(f32[128,128]{1,0:T(8,128)S(1)} %cholesky.621), custom_call_target="Cholesky" | custom-call | tf_op jit(solution)/shard_map/jit(cholesky)/cholesky | solution.py:24
  737.8 9.8 %custom-call.58 = f32[1,128,128]{1,2,0:T(8,128)S(1)} custom-call(f32[1,128,128]{2,1,0:T(8,128)S(1)} %get-tuple-element.327), custom_call_target="InvertDiagBlocksLowerTriangular" | custom-call | tf_op jit(solution)/shard_map/jit(cholesky)/cholesky | solution.py:24
  749.3 11.9 %cholesky.575 = f32[128,128]{1,0:T(8,128)S(1)} custom-call(f32[128,128]{1,0:T(8,128)S(1)} %convolution_subtract_fusion.30), custom_call_target="Cholesky" | custom-call | tf_op jit(solution)/shard_map/jit(cholesky)/cholesky | solution.py:24
  771.7 12.0 %while.29 = (s32[]{:T(128)}, f32[512,512]{0,1:T(8,128)}, s32[4,2]{0,1:T(2,128)S(1)}, f32[4,128,128]{2,1,0:T(8,128)S(1)}, s32[]{:T(128)}) while((s32[]{:T(128)}, f32[512,512]{0,1:T(8,128)}, s32[4,2]{0,1:T(2,128)S(1)}, f32[4,128,128]{2,1,0:T(8,128)S(1)}, s32[]{:T(128)}) %tuple.216), condition=%wide.while_cond.1.clone.1, body=%wide.while_body.1.clone.1.sunk | while | flops 2 | bytes 393321 | solution.py:27
  783.7 39.3 %custom-call.60 = f32[4,128,128]{1,2,0:T(8,128)S(1)} custom-call(f32[4,128,128]{2,1,0:T(8,128)S(1)} %get-tuple-element.95), custom_call_target="InvertDiagBlocksLowerTriangular" | custom-call | tf_op jit(solution)/shard_map/triangular_solve/custom-call.8 | solution.py:27
  831.4 12.0 %while.28 = (s32[]{:T(128)}, f32[512,512]{0,1:T(8,128)}, s32[4,2]{0,1:T(2,128)S(1)}, f32[4,128,128]{2,1,0:T(8,128)S(1)}, s32[]{:T(128)}) while((s32[]{:T(128)}, f32[512,512]{0,1:T(8,128)}, s32[4,2]{0,1:T(2,128)S(1)}, f32[4,128,128]{2,1,0:T(8,128)S(1)}, s32[]{:T(128)}) %tuple.217), condition=%wide.while_cond.clone.1, body=%wide.while_body.clone.1.sunk | while | flops 2 | bytes 393321 | solution.py:26
  843.4 39.6 %custom-call.59 = f32[4,128,128]{1,2,0:T(8,128)S(1)} custom-call(f32[4,128,128]{2,1,0:T(8,128)S(1)} %get-tuple-element.94), custom_call_target="InvertDiagBlocksLowerTriangular" | custom-call | tf_op jit(solution)/shard_map/triangular_solve/custom-call.3 | solution.py:26
  (427 shorter events, 216.0 us)
Async XLA Ops:
  7.2 61.5 %all-reduce.8.cloned.1.call-start = ((), (), s32[]{:S(2)}) async-start(), calls=%async_computation | async-start | bytes 262144 | tf_op jit(solution)/shard_map/psum | solution.py:18
  12.8 336.0 %all-reduce.10.cloned.1.call-start = ((), (), s32[]{:S(2)}) async-start(), calls=%async_computation.1 | async-start | bytes 262144 | tf_op jit(solution)/shard_map/psum | solution.py:18
  49.4 2.6 copy-start.23
  85.4 1.0 copy-start.6
  240.9 41.6 %copy-start.10 = (f32[2,128,256]{2,1,0:T(8,128)S(1)}, f32[2,128,256]{2,1,0:T(8,128)}, u32[]{:S(2)}) copy-start(f32[2,128,256]{2,1,0:T(8,128)} %param.22) | copy-start | bytes 786436
  286.1 1.7 copy-start.3
  287.1 170.5 %copy-start.4 = (f32[256,256]{1,0:T(8,128)}, f32[256,256]{1,0:T(8,128)S(1)}, u32[]{:S(2)}) copy-start(f32[256,256]{1,0:T(8,128)S(1)} %convolution_subtract_fusion.5) | copy-start | bytes 786436
  291.2 4.4 copy-start.22
  294.8 298.9 %copy-start = (f32[1024,256]{1,0:T(8,128)}, f32[1024,256]{1,0:T(8,128)S(1)}, u32[]{:S(2)}) copy-start(f32[1024,256]{1,0:T(8,128)S(1)} %convolution_subtract_fusion.2) | copy-start | bytes 3145732
  295.5 357.9 %all-reduce.12.cloned.1.call-start = ((), (), s32[]{:S(2)}) async-start(), calls=%async_computation.2 | async-start | bytes 262144 | tf_op jit(solution)/shard_map/psum | solution.py:18
  295.6 11.9 %copy-start.17 = (f32[256]{0:T(256)}, f32[256]{0:T(256)S(1)}, u32[]{:S(2)}) copy-start(f32[256]{0:T(256)S(1)} %bitcast_subtract_fusion) | copy-start | bytes 3076
  368.0 1.0 copy-start.7
  393.7 12.3 %copy-start.12 = (f32[384,128]{1,0:T(8,128)}, f32[384,128]{1,0:T(8,128)S(1)}, u32[]{:S(2)}) copy-start(f32[384,128]{1,0:T(8,128)S(1)} %convolution_subtract_fusion.7) | copy-start | bytes 589828
  407.2 50.0 %copy-start.15 = (f32[256,4]{1,0:T(8,128)S(1)}, f32[256,4]{1,0:T(8,128)}, u32[]{:S(2)}) copy-start(f32[256,4]{1,0:T(8,128)} %copy.118) | copy-start | bytes 12292
  457.2 3.6 copy-start.24
  457.3 4.3 copy-start.26
  479.2 49.9 %copy-start.2 = (f32[512,512]{0,1:T(8,128)S(1)}, f32[512,512]{0,1:T(8,128)}, u32[]{:S(2)}) copy-start(f32[512,512]{0,1:T(8,128)} %get-tuple-element.584) | copy-start | bytes 3145732
  525.1 4.0 copy-start.11
  581.0 5.4 copy-start.9
  582.3 9.9 %copy-start.5 = (f32[256,256]{1,0:T(8,128)S(1)}, f32[256,256]{1,0:T(8,128)}, u32[]{:S(2)}) copy-start(f32[256,256]{1,0:T(8,128)} %copy-done.4) | copy-start | bytes 786436
  595.7 1.9 copy-start.1
  597.6 2.5 copy-start.18
  597.6 2.6 copy-start.28
  600.2 31.9 %copy-start.19 = (f32[256]{0:T(256)}, f32[256]{0:T(256)S(1)}, u32[]{:S(2)}) copy-start(f32[256]{0:T(256)S(1)} %sub.53) | copy-start | bytes 3076
  672.8 1.0 copy-start.8
  698.4 12.4 %copy-start.13 = (f32[384,128]{1,0:T(8,128)}, f32[384,128]{1,0:T(8,128)S(1)}, u32[]{:S(2)}) copy-start(f32[384,128]{1,0:T(8,128)S(1)} %convolution_subtract_fusion.6) | copy-start | bytes 589828
  711.8 50.0 %copy-start.14 = (f32[256,4]{1,0:T(8,128)S(1)}, f32[256,4]{1,0:T(8,128)}, u32[]{:S(2)}) copy-start(f32[256,4]{1,0:T(8,128)} %copy.139) | copy-start | bytes 12292
  761.8 3.6 copy-start.25
  761.9 4.3 copy-start.27
  769.4 53.7 %copy-start.16 = (f32[4,1,128]{2,1,0:T(1,128)S(1)}, f32[4,1,128]{2,1,0:T(1,128)}, u32[]{:S(2)}) copy-start(f32[4,1,128]{2,1,0:T(1,128)} %all-gather.5) | copy-start | bytes 6148
  898.9 2.8 copy-start.20
  898.9 3.4 copy-start.21
Sparse Core Ops, SparseCore 0:
  12.9 55.6 all-reduce.7
  295.7 53.0 all-reduce.9
  600.3 53.0 all-reduce.11
where the time goes:
time: 922 us; the launch traced here: 910 us
  other arithmetic  499 us (54%)
  blocking collectives  142 us (15%)
  matrix products  96.5 us (10%)
  local copies, waits for them, and re-layouts  88.8 us (10%)
  waiting for transfers between devices  49.8 us (5%)
  between operations  33.2 us (4%)
    another operation x44, other arithmetic, factorize(): lower_factor = jnp.linalg.cholesky(system)  244 us
    another operation x7, other arithmetic, factorize(): lax.linalg.triangular_solve(lower_factor, solved, left_side=True, lower=T...  126 us
    another operation x3, other arithmetic, factorize(): lax.linalg.triangular_solve(shifted, anomalies, left_side=True, lower=True)  119 us
    psum x3, waiting for transfers between devices, from_root(): return lax.psum(block, axis)  49.7 us
    all_gather x3, blocking collectives, per_device(): lax.all_gather(sent_rows, 'shard', axis=0, tiled=True)  46.1 us
    psum x3, blocking collectives, from_root(): return lax.psum(block, axis)  38.7 us
    another operation x60, local copies, waits for them, and re-layouts, factorize(): lax.linalg.triangular_solve(shifted, anomalies, left_side=True, lower=True)  35.7 us
    all_gather x3, blocking collectives, per_device(): lax.all_gather(sent_var, 'shard', axis=0, tiled=True)  34.3 us
  transfers between devices with their start and end apart: 3, of which 3 were waited for; matrix products, arithmetic and copies ran while one was open for 1% of the time, Pallas kernels for 0%

commit v1 on v0

v1 whole, which is shorter than its diff:
```python
import jax
import jax.numpy as jnp
from jax import lax
from jax.experimental import pallas as pl
from jax.experimental.pallas import tpu as pltpu
from jax.sharding import PartitionSpec as P

TAPER_BLOCK = 128
LANES = 128
PANEL = 16
highest = lax.Precision.HIGHEST
f32 = jnp.float32
bf16 = jnp.bfloat16


def dot(a, b, dims=((1,), (0,))):
    return lax.dot_general(a, b, (dims, ((), ())), precision=highest, preferred_element_type=f32)


def split2(x):
    hi = x.astype(bf16)
    return hi, (x - hi.astype(f32)).astype(bf16)


def split3(x):
    hi = x.astype(bf16).astype(f32)
    rest = x - hi
    mid = rest.astype(bf16).astype(f32)
    return hi, mid, rest - mid


def dot3(a, b_hi, b_lo, dims=((1,), (0,))):
    hi, lo = split2(a)

    def one(u, v):
        return lax.dot_general(u, v, (dims, ((), ())), preferred_element_type=f32)

    return one(hi, b_hi) + (one(hi, b_lo) + one(lo, b_hi))


def factor_block(sgh, roots):
    rows = lax.broadcasted_iota(jnp.int32, (PANEL, LANES), 0)
    for start in range(0, TAPER_BLOCK, PANEL):
        panel = sgh[start : start + PANEL, :]
        cols = [
            jnp.broadcast_to(panel[:, start + t : start + t + 1], (PANEL, LANES))
            for t in range(PANEL)
        ]
        parts = [panel[:, LANES * q : LANES * (q + 1)] for q in range(3)]
        root = roots[start : start + PANEL, :]
        for r in range(PANEL):
            pivot = cols[r][r : r + 1, :]
            inv = lax.rsqrt(pivot)
            column = cols[r] * inv
            for t in range(r + 1, PANEL):
                cols[t] = cols[t] - column * column[t : t + 1, :]
            below = jnp.where(rows > r, column, 0.0)
            shifted = 1.0 / (pivot * inv + root[r : r + 1, :])
            for q, scale in enumerate((inv, inv, shifted)):
                done = parts[q][r : r + 1, :] * scale
                parts[q] = jnp.where(rows == r, done, parts[q] - below * done)
        solved = jnp.concatenate(parts, axis=1)
        sgh[start : start + PANEL, :] = solved
        after = start + PANEL
        if after < TAPER_BLOCK:
            a, b, c = split3(parts[0])
            left = jnp.concatenate([a, a, b, a, b, c, jnp.zeros((32, LANES), f32)], axis=0)
            x, y, z = (v.astype(bf16) for v in split3(solved))
            right = jnp.concatenate([x, y, x, z, y, x, jnp.zeros((32, 3 * LANES), bf16)], axis=0)
            left = left.T[after:, :].astype(bf16)
            sgh[after:, :] = sgh[after:, :] - jnp.dot(left, right, preferred_element_type=f32)


def analysis_kernel(
    members, state_in, obs_in, batch_in, tw_state, tw_obs, tw_batch, state, obs, batch, work, sgh, roots, inverses, y_hi, y_lo, z, z_hi, z_lo
):
    steps, size, width = batch_in.shape
    blocks = size // TAPER_BLOCK
    state[...] = state_in[...]
    obs[...] = obs_in[...]
    for k in range(steps):
        batch[k] = batch_in[k]
    eye = (
        lax.broadcasted_iota(jnp.int32, (TAPER_BLOCK, LANES), 0)
        == lax.broadcasted_iota(jnp.int32, (TAPER_BLOCK, LANES), 1)
    ).astype(f32)
    lane = lax.broadcasted_iota(jnp.int32, (TAPER_BLOCK, LANES), 1)
    extra = size + members

    def one_batch(k, carry):
        y = batch[k, :, :members]
        hi, lo = split2(y)
        y_hi[...] = hi
        y_lo[...] = lo
        work[:, size:] = batch[k]
        for j in range(blocks):
            here = y[j * TAPER_BLOCK : (j + 1) * TAPER_BLOCK]
            work[j * TAPER_BLOCK : (j + 1) * TAPER_BLOCK, :size] = dot(here, y, ((1,), (1,))) / (members - 1)

        def eliminate(j, carry):
            top = pl.multiple_of(j * TAPER_BLOCK, TAPER_BLOCK)
            mine = pl.ds(top, TAPER_BLOCK)
            variance = jnp.broadcast_to(batch[k, mine, members + 1 : members + 2], (TAPER_BLOCK, LANES))
            roots[...] = jnp.sqrt(variance)
            sgh[:, :LANES] = work[mine, mine] + eye * variance
            sgh[:, LANES : 2 * LANES] = eye
            sgh[:, 2 * LANES :] = eye
            factor_block(sgh, roots)
            inverse = sgh[:, LANES : 2 * LANES]
            inverses[j] = inverse
            work[mine, :size] = dot(inverse, work[mine, :size])
            work[mine, size:extra] = dot(sgh[:, 2 * LANES :], work[mine, size:extra])
            work[mine, extra:] = dot(inverse, work[mine, extra:])

            def trail(i, carry):
                lower = pl.ds(pl.multiple_of(i * TAPER_BLOCK, TAPER_BLOCK), TAPER_BLOCK)
                work[lower, :] = work[lower, :] - dot(work[mine, lower].T, work[mine, :])
                return carry

            return lax.fori_loop(j + 1, blocks, trail, carry)

        lax.fori_loop(0, blocks, eliminate, 0)

        def back(step, carry):
            j = blocks - 1 - step
            mine = pl.ds(pl.multiple_of(j * TAPER_BLOCK, TAPER_BLOCK), TAPER_BLOCK)

            def gather(i, acc):
                lower = pl.ds(pl.multiple_of(i * TAPER_BLOCK, TAPER_BLOCK), TAPER_BLOCK)
                return acc - dot(work[mine, lower], z[lower, :])

            acc = lax.fori_loop(j + 1, blocks, gather, work[mine, size:])
            z[mine, :] = dot(inverses[j].T, acc)
            return carry

        lax.fori_loop(0, blocks, back, 0)
        for j in range(blocks):
            mine = slice(j * TAPER_BLOCK, (j + 1) * TAPER_BLOCK)
            tail = jnp.where(lane == 0, z[mine, members:], 0.0)
            full = jnp.concatenate([z[mine, :members], tail], axis=1)
            hi, lo = split2(full)
            z_hi[mine, :] = hi
            z_lo[mine, :] = lo

        def updated(x, weights):
            covar = dot3(x[:, :members], y_hi[...], y_lo[...], ((1,), (1,))) * weights
            return x - dot3(covar, z_hi[...], z_lo[...])

        def state_block(i, carry):
            mine = pl.ds(pl.multiple_of(i * TAPER_BLOCK, TAPER_BLOCK), TAPER_BLOCK)
            state[mine, :] = updated(state[mine, :], tw_state[k, pl.ds(i, 1), :])
            return carry

        lax.fori_loop(0, state.shape[0] // TAPER_BLOCK, state_block, 0)
        groups = tw_obs.shape[1]
        high = obs.shape[0] // groups
        for g in range(groups):
            mine = slice(g * high, (g + 1) * high)
            obs[mine, :] = updated(obs[mine, :], tw_obs[k, g : g + 1, :])

        def later(i, carry):
            which = i // blocks
            mine = pl.ds(pl.multiple_of(lax.rem(i, blocks) * TAPER_BLOCK, TAPER_BLOCK), TAPER_BLOCK)
            batch[which, mine, :] = updated(batch[which, mine, :], tw_batch[k, pl.ds(i, 1), :])
            return carry

        lax.fori_loop((k + 1) * blocks, steps * blocks, later, 0)
        return carry

    lax.fori_loop(0, steps, one_batch, 0)


def analyse(members, state, obs, batch, tw_state, tw_obs, tw_batch):
    steps, size, width = batch.shape
    blocks = size // TAPER_BLOCK
    vmem = pl.BlockSpec(memory_space=pltpu.VMEM)

    def kernel(*refs):
        analysis_kernel(members, *refs)

    return pl.pallas_call(
        kernel,
        out_shape=(jax.ShapeDtypeStruct(state.shape, f32), jax.ShapeDtypeStruct(obs.shape, f32)),
        in_specs=[vmem] * 6,
        out_specs=(vmem, vmem),
        scratch_shapes=[
            pltpu.VMEM(batch.shape, f32),
            pltpu.VMEM((size, size + width), f32),
            pltpu.VMEM((TAPER_BLOCK, 3 * LANES), f32),
            pltpu.VMEM((TAPER_BLOCK, LANES), f32),
            pltpu.VMEM((blocks, TAPER_BLOCK, LANES), f32),
            pltpu.VMEM((size, members), bf16),
            pltpu.VMEM((size, members), bf16),
            pltpu.VMEM((size, width), f32),
            pltpu.VMEM((size, width), bf16),
            pltpu.VMEM((size, width), bf16),
        ],
        compiler_params=pltpu.CompilerParams(vmem_limit_bytes=48 * 1024 * 1024),
    )(state, obs, batch, tw_state, tw_obs, tw_batch)


def lookup(levels, index):
    onehot = (index[..., None] == jnp.arange(levels.shape[0], dtype=jnp.int32)).astype(f32)
    return jnp.sum(onehot * levels, axis=-1)


def per_device(
    state_anom, state_mean, obs_anom, obs_depart, obs_var, taper_levels, state_taper, obs_taper, batch_order
):
    region, shard = lax.axis_index("region"), lax.axis_index("shard")
    per_region, pieces, members = obs_anom.shape
    steps = batch_order.shape[0]
    size = pieces * lax.axis_size("shard")
    blocks = size // TAPER_BLOCK

    def columns(weights):
        return jnp.repeat(weights, TAPER_BLOCK, axis=-1) / (members - 1)

    wanted = (batch_order[:, None] * blocks + jnp.arange(blocks, dtype=jnp.int32)).reshape(-1)
    state_weights = lookup(taper_levels, jnp.take(state_taper, wanted, axis=1))
    tw_state = columns(state_weights.reshape(-1, steps, blocks)).transpose(1, 0, 2)
    obs_weights = lookup(taper_levels, jnp.take(obs_taper, wanted, axis=1))
    high = min(pieces, TAPER_BLOCK)
    group_rows = jnp.arange(per_region * pieces // high, dtype=jnp.int32) * high
    group_block = (group_rows // pieces * size + shard * pieces + group_rows % pieces) // TAPER_BLOCK
    mine = jnp.take(obs_weights, group_block, axis=0)
    tw_obs = columns(mine.reshape(-1, steps, blocks)).transpose(1, 0, 2)

    weight_rows = jnp.repeat(mine, high, axis=0).reshape(per_region, pieces, steps * blocks)
    pad = jnp.zeros((per_region, pieces, LANES - 2 - steps * blocks), f32)
    table = jnp.concatenate([obs_anom, obs_depart[..., None], obs_var[..., None], weight_rows, pad], axis=-1)
    share = jnp.take(table, batch_order % per_region, axis=0)
    owned = (batch_order // per_region == region)[:, None, None]
    share = lax.psum(jnp.where(owned, share, 0.0), "region")
    batch = lax.all_gather(share, "shard", axis=1, tiled=True)

    between = batch[:, ::TAPER_BLOCK, members + 2 : members + 2 + steps * blocks]
    tw_batch = columns(between.reshape(steps * blocks, steps, blocks)).transpose(1, 0, 2)

    def widened(rows, column):
        pad = jnp.zeros((rows.shape[0], LANES - 1), f32)
        return jnp.concatenate([rows, column[:, None], pad], axis=1)

    state, obs = analyse(
        members,
        widened(state_anom, -state_mean),
        widened(obs_anom.reshape(-1, members), obs_depart.reshape(-1)),
        batch,
        tw_state,
        tw_obs,
        tw_batch,
    )
    return (
        state[:, :members],
        -state[:, members],
        obs[:, :members].reshape(obs_anom.shape),
        obs[:, members].reshape(obs_depart.shape),
    )


def solution(mesh):
    placed = (
        P(("region", "shard"), None),
        P(("region", "shard")),
        P("region", "shard", None),
        P("region", "shard"),
        P("region", "shard"),
        P(),
        P(("region", "shard"), None),
        P("region", None),
        P(),
    )
    return jax.shard_map(
        per_device,
        mesh=mesh,
        in_specs=placed,
        out_specs=(
            P(("region", "shard"), None),
            P(("region", "shard")),
            P("region", "shard", None),
            P("region", "shard"),
        ),
        check_vma=False,
    )
```

time: 922 us -> 248 us (0.27); the launches traced: 910 us -> 248 us
  other arithmetic: 499 us -> 5.62 us
  blocking collectives: 142 us -> 0 us
  Pallas kernels: 0 us -> 110 us
  matrix products: 96.5 us -> 0 us
  local copies, waits for them, and re-layouts: 88.8 us -> 11.5 us
  waiting for transfers between devices: 49.8 us -> 107 us
  between operations: 33.2 us -> 14.2 us
    another operation x54 -> x0, other arithmetic: 489 us -> none  [the longest x44 244 us: factorize(): lower_factor = jnp.linalg.cholesky(system)]
    pallas_call x0 -> x1, Pallas kernels: none -> 110 us  [analyse(): pl.pallas_call(kernel, out_shape=(jax.ShapeDtypeStruct(state.shape, f32),...]
    all_gather x9 -> x0, blocking collectives: 103 us -> none  [the longest x3 46.1 us: per_device(): lax.all_gather(sent_rows, 'shard', axis=0, tiled=True)]
    another operation x166 -> x1, local copies, waits for them, and re-layouts: 73.3 us -> 0.13 us  [widened(): return jnp.concatenate([rows, column[:, None], pad], axis=1)]
    another operation x102 -> x0, matrix products: 67.7 us -> none  [the longest x18 19.6 us: factorize(): lower_factor = jnp.linalg.cholesky(system)]
    all_gather x0 -> x1, waiting for transfers between devices: none -> 49.1 us  [per_device(): batch = lax.all_gather(share, 'shard', axis=1, tiled=True)]
    psum x3 -> x0, blocking collectives: 38.7 us -> none  [from_root(): return lax.psum(block, axis)]
    dot_general x21 -> x0, matrix products: 28.8 us -> none  [the longest x6 11.2 us: apply_rows(): jnp.dot(covar, increments, precision=highest, preferred_element_type=jnp....]
  transfers between devices with their start and end apart: 3 -> 2, of which waited for: 3 -> 2; matrix products, arithmetic and copies ran while one was open for 1% -> 1% of each run, Pallas kernels for 0% -> 0%
where the time goes in v1:
time: 248 us
  Pallas kernels  110 us (44%)
  waiting for transfers between devices  107 us (43%)
  between operations  14.2 us (6%)
  local copies, waits for them, and re-layouts  11.5 us (5%)
  other arithmetic  5.62 us (2%)
    pallas_call x1, Pallas kernels, analyse(): pl.pallas_call(kernel, out_shape=(jax.ShapeDtypeStruct(state.shape, f32),...  110 us
    psum x1, waiting for transfers between devices, per_device(): share = lax.psum(jnp.where(owned, share, 0.0), 'region')  57.7 us
    all_gather x1, waiting for transfers between devices, per_device(): batch = lax.all_gather(share, 'shard', axis=1, tiled=True)  49.1 us
  transfers between devices with their start and end apart: 2, of which 2 were waited for; matrix products, arithmetic and copies ran while one was open for 1% of the time, Pallas kernels for 0%

profile of v1, /device:TPU:0, one launch (start us, length us, event | category | flops | bytes accessed | tf_op | source)
XLA Modules:
  0.0 248.0 jit_solution(3497435176534951878)
XLA Ops:
  7.2 0.0 all-reduce.2.cloned.1.call-start
  7.3 0.7 broadcast_multiply_fusion.2
  7.9 0.1 iota_add_fusion
  8.0 0.1 add.128
  8.1 0.7 compare_and_fusion.2
  8.8 0.8 copy.37
  9.6 0.8 copy.33
  10.4 0.6 gather_fusion.3
  10.9 0.6 gather_fusion.2
  11.5 0.1 select_bitcast_fusion.1
  11.6 0.1 copy.34
  11.6 0.1 copy.38
  11.7 0.8 copy.36
  12.5 0.8 copy.35
  13.4 0.8 select_reduce_fusion
  14.1 0.6 gather_fusion
  14.7 0.1 broadcast_select_fusion
  14.8 1.1 concatenate.11
  15.9 0.0 copy-start.2
  15.9 0.0 copy-start.1
  15.9 0.6 gather_fusion.1
  16.5 0.0 copy-start
  16.5 0.9 select_select_fusion
  17.5 0.0 all-reduce.2.cloned.1.call-update
  17.5 0.0 all-gather.2.cloned.1.call-start
  17.6 57.7 %all-reduce.2.cloned.1.call-done = f32[3,128,384]{2,1,0:T(8,128)} async-done(((f32[3,128,384]{2,1,0:T(8,128)}), f32[3,128,384]{2,1,0:T(8,128)}) %all-reduce.2.cloned.1.call-update) | async-done | bytes 589840 | tf_op jit(solution)/shard_map/psum | solution.py:234
  75.3 0.0 all-gather.2.cloned.1.call-update
  75.3 0.1 gather.15
  75.4 0.0 copy-done.2
  75.4 0.1 select_multiply_fusion
  75.5 0.1 copy.39
  75.6 0.1 broadcast_in_dim.95
  75.7 0.0 copy-done.1
  75.7 0.1 copy.32
  75.8 0.2 copy.31
  76.1 0.1 pad.5.clone
  76.1 0.1 broadcast_bitcast_fusion.refs_3_
  76.2 0.0 copy-done
  76.3 1.4 maximum_maximum_fusion.refs_0_
  77.6 49.1 %all-gather.2.cloned.1.call-done.refs_2_ = f32[3,512,384]{2,1,0:T(8,128)} async-done(((f32[3,128,384]{2,1,0:T(8,128)}), f32[3,512,384]{2,1,0:T(8,128)}) %all-gather.2.cloned.1.call-update) | async-done | bytes 2359312 | tf_op jit(solution)/shard_map/all_gather | solution.py:235
  126.7 1.2 slice.15
  128.0 0.1 div.98
  128.1 0.1 broadcast_in_dim.96
  128.2 109.7 %shard_map.120 = (f32[1024,384]{1,0:T(8,128)S(1)}, f32[256,384]{1,0:T(8,128)S(1)}) custom-call(f32[1024,384]{1,0:T(8,128)S(1)} %maximum_maximum_fusion.refs_0_, f32[256,384]{1,0:T(8,128)S(1)} %maximum_maximum_fusion.1.refs_1_, f32[3,512,384]{2,1,0:T(8,128)} %all-gather.2.cloned.1.call-done.refs_2_, f32[3,8,512]{2,1,0:T(8,128)S(1)} %broadcast_bitcast_fusion.refs_3_, ...), custom_call_target="tpu_custom_call" | custom-call | tf_op jit(solution)/shard_map/pallas_call | solution.py:181
  237.9 0.7 slice_reduce_fusion
  238.6 0.7 slice.18
  239.3 0.8 negate_reduce_fusion
  240.1 1.1 slice.16
  (19 shorter events, 0.2 us)
Async XLA Ops:
  7.2 68.1 %all-reduce.2.cloned.1.call-start = ((), (), s32[]{:S(2)}) async-start(), calls=%async_computation | async-start | bytes 1179648 | tf_op jit(solution)/shard_map/psum | solution.py:234
  15.9 59.5 %copy-start.2 = (f32[1024]{0:T(1024)S(1)}, f32[1024]{0:T(1024)}, u32[]{:S(2)}) copy-start(f32[1024]{0:T(1024)} %param.12) | copy-start | bytes 12292
  15.9 59.8 %copy-start.1 = (f32[2,128]{1,0:T(2,128)S(1)}, f32[2,128]{1,0:T(2,128)}, u32[]{:S(2)}) copy-start(f32[2,128]{1,0:T(2,128)} %param.14) | copy-start | bytes 3076
  16.5 59.7 %copy-start = (f32[2,128,256]{2,1,0:T(8,128)S(1)}, f32[2,128,256]{2,1,0:T(8,128)}, u32[]{:S(2)}) copy-start(f32[2,128,256]{2,1,0:T(8,128)} %param.13) | copy-start | bytes 786436
  17.5 109.2 %all-gather.2.cloned.1.call-start = ((), (), s32[]{:S(2)}) async-start(), calls=%async_computation.1 | async-start | bytes 2949120 | tf_op jit(solution)/shard_map/all_gather | solution.py:235
Sparse Core Ops, SparseCore 0:
  17.6 57.6 all-reduce.1
  76.9 49.7 all-gather.1

commit v2 on v1

--- a/solution.py
+++ b/solution.py
@@ -199,6 +199,84 @@
     )(state, obs, batch, tw_state, tw_obs, tw_batch)
 
 
+def spread_kernel(mesh_axes, share, out, landed, *sems):
+    (sum_send, sum_recv, shard_send, shard_recv, peer_send, peer_recv, pair_send, pair_recv) = sems
+    regions, shards = (lax.axis_size(name) for name in mesh_axes)
+    g, s = (lax.axis_index(name) for name in mesh_axes)
+    half = regions // 2
+    pair = g + 1 - 2 * lax.rem(g, 2)
+
+    def copy(src, dst, send, recv, device):
+        return pltpu.make_async_remote_copy(
+            src_ref=src, dst_ref=dst, send_sem=send, recv_sem=recv, device_id=device, device_id_type=pl.DeviceIdType.MESH
+        )
+
+    barrier = pltpu.get_barrier_semaphore()
+    for o in range(1, regions):
+        pl.semaphore_signal(barrier, inc=1, device_id=(lax.rem(g + o, regions), s), device_id_type=pl.DeviceIdType.MESH)
+    for o in range(1, shards):
+        pl.semaphore_signal(barrier, inc=1, device_id=(g, lax.rem(s + o, shards)), device_id_type=pl.DeviceIdType.MESH)
+    pl.semaphore_wait(barrier, regions + shards - 2)
+
+    sums = []
+    for o in range(1, regions):
+        to = lax.rem(g + o, regions)
+        sums.append(copy(share.at[to], landed.at[o - 1], sum_send.at[o - 1], sum_recv.at[o - 1], (to, s)))
+        sums[-1].start()
+    total = share[g]
+    for o in range(1, regions):
+        sums[o - 1].wait_recv()
+        total = total + landed[o - 1]
+    out[g, s] = total
+
+    along = []
+    for o in range(1, shards):
+        to = lax.rem(s + o, shards)
+        along.append(copy(out.at[g, s], out.at[g, s], shard_send.at[o - 1], shard_recv.at[o - 1], (g, to)))
+        along[-1].start()
+    for c in along:
+        c.wait_recv()
+
+    peers = []
+    for o in range(1, half):
+        to = lax.rem(g + 2 * o, regions)
+        peers.append(copy(out.at[g], out.at[g], peer_send.at[o - 1], peer_recv.at[o - 1], (to, s)))
+        peers[-1].start()
+    pairs = [copy(out.at[g], out.at[g], pair_send.at[0], pair_recv.at[0], (pair, s))]
+    pairs[0].start()
+    for o in range(1, half):
+        peers[o - 1].wait_recv()
+        source = lax.rem(g + regions - 2 * o, regions)
+        pairs.append(copy(out.at[source], out.at[source], pair_send.at[o], pair_recv.at[o], (pair, s)))
+        pairs[-1].start()
+    for c in pairs:
+        c.wait_recv()
+    for c in sums + along + peers + pairs:
+        c.wait_send()
+
+
+def spread(share):
+    axes = ("region", "shard")
+    regions, shards = (lax.axis_size(name) for name in axes)
+    counts = (regions - 1, regions - 1, shards - 1, shards - 1, regions // 2 - 1, regions // 2 - 1, regions // 2, regions // 2)
+    vmem = pl.BlockSpec(memory_space=pltpu.VMEM)
+
+    def kernel(*refs):
+        spread_kernel(axes, *refs)
+
+    return pl.pallas_call(
+        kernel,
+        out_shape=jax.ShapeDtypeStruct((regions, shards) + share.shape[1:], f32),
+        in_specs=[vmem],
+        out_specs=vmem,
+        scratch_shapes=[pltpu.VMEM((regions - 1,) + share.shape[1:], f32)]
+        + [pltpu.SemaphoreType.DMA((n,)) for n in counts],
+        compiler_params=pltpu.CompilerParams(
+            collective_id=0, has_side_effects=True, vmem_limit_bytes=32 * 1024 * 1024
+        ),
+    )(share)
+
+
 def lookup(levels, index):
     onehot = (index[..., None] == jnp.arange(levels.shape[0], dtype=jnp.int32)).astype(f32)
     return jnp.sum(onehot * levels, axis=-1)
@@ -226,15 +304,34 @@
     mine = jnp.take(obs_weights, group_block, axis=0)
     tw_obs = columns(mine.reshape(-1, steps, blocks)).transpose(1, 0, 2)
 
-    weight_rows = jnp.repeat(mine, high, axis=0).reshape(per_region, pieces, steps * blocks)
-    pad = jnp.zeros((per_region, pieces, LANES - 2 - steps * blocks), f32)
-    table = jnp.concatenate([obs_anom, obs_depart[..., None], obs_var[..., None], weight_rows, pad], axis=-1)
+    regions, shards = lax.axis_size("region"), lax.axis_size("shard")
+    halves = members // LANES
+
+    def filled(rows):
+        return jnp.pad(rows, ((0, 0), (0, LANES - rows.shape[1])))[:, None]
+
+    first_group = mine[:: pieces // high]
+    small = jnp.concatenate(
+        [filled(obs_depart), filled(obs_var), filled(first_group), jnp.zeros((per_region, 5, LANES), f32)], axis=1
+    )
+    table = jnp.concatenate([obs_anom[:, :, h * LANES : (h + 1) * LANES] for h in range(halves)] + [small], axis=1)
     share = jnp.take(table, batch_order % per_region, axis=0)
     owned = (batch_order // per_region == region)[:, None, None]
-    share = lax.psum(jnp.where(owned, share, 0.0), "region")
-    batch = lax.all_gather(share, "shard", axis=1, tiled=True)
-
-    between = batch[:, ::TAPER_BLOCK, members + 2 : members + 2 + steps * blocks]
+    share = jnp.where(owned, share, 0.0).reshape(-1, LANES)
+    per_step = halves * pieces + 8
+    chunk = -(-steps * per_step // (8 * regions)) * 8
+    share = jnp.pad(share, ((0, chunk * regions - steps * per_step), (0, 0))).reshape(regions, chunk, LANES)
+    spreaded = spread(share).transpose(1, 0, 2, 3).reshape(shards, regions * chunk, LANES)
+    spreaded = spreaded[:, : steps * per_step].reshape(shards, steps, per_step, LANES)
+    anomalies = [
+        spreaded[:, :, h * pieces : (h + 1) * pieces].transpose(1, 0, 2, 3).reshape(steps, size, LANES)
+        for h in range(halves)
+    ]
+    small = spreaded[:, :, halves * pieces :]
+    columns_in = small[:, :, :2, :pieces].transpose(1, 0, 3, 2).reshape(steps, size, 2)
+    batch = jnp.concatenate(anomalies + [jnp.pad(columns_in, ((0, 0), (0, 0), (0, LANES - 2)))], axis=-1)
+
+    between = small[:: TAPER_BLOCK // pieces, :, 2, : steps * blocks].transpose(1, 0, 2)
     tw_batch = columns(between.reshape(steps * blocks, steps, blocks)).transpose(1, 0, 2)
 
     def widened(rows, column):

time: 248 us -> 159 us (0.64)
  waiting for transfers between devices: 107 us -> 0 us
  Pallas kernels: 110 us -> 139 us
  between operations: 14.2 us -> 0.88 us
    psum x1 -> x0, waiting for transfers between devices: 57.7 us -> none  [per_device(): share = lax.psum(jnp.where(owned, share, 0.0), 'region')]
    all_gather x1 -> x0, waiting for transfers between devices: 49.1 us -> none  [per_device(): batch = lax.all_gather(share, 'shard', axis=1, tiled=True)]
    pallas_call x0 -> x1, Pallas kernels: none -> 29.4 us  [spread(): pl.pallas_call(kernel, out_shape=jax.ShapeDtypeStruct((regions, shards) +...]
    concatenate x0 -> x1, other arithmetic: none -> 2.71 us  [per_device(): jnp.concatenate(anomalies + [jnp.pad(columns_in, ((0, 0), (0, 0), (0, LAN...]
  transfers between devices with their start and end apart: 2 -> 0, of which waited for: 2 -> 0; matrix products, arithmetic and copies ran while one was open for 1% -> 0% of each run, Pallas kernels for 0% -> 0%
where the time goes in v2:
time: 159 us
  Pallas kernels  139 us (87%)
  local copies, waits for them, and re-layouts  11.3 us (7%)
  other arithmetic  7.72 us (5%)
    pallas_call x1, Pallas kernels, analyse(): pl.pallas_call(kernel, out_shape=(jax.ShapeDtypeStruct(state.shape, f32),...  110 us
    pallas_call x1, Pallas kernels, spread(): pl.pallas_call(kernel, out_shape=jax.ShapeDtypeStruct((regions, shards) +...  29.4 us

profile of v2, /device:TPU:0, one launch (start us, length us, event | category | flops | bytes accessed | tf_op | source)
XLA Modules:
  0.0 159.1 jit_solution(13871191264531418826)
XLA Ops:
  0.6 0.7 broadcast_multiply_fusion.1
  1.3 0.1 iota_add_fusion
  1.4 0.1 add.132
  1.5 0.8 copy.59
  2.2 0.6 gather_fusion.2
  2.8 0.8 copy.68
  3.6 0.6 gather_fusion.3
  4.1 0.1 select_bitcast_fusion.1
  4.2 0.1 copy.60
  4.3 0.1 copy.69
  4.4 0.7 select_reduce_fusion
  5.2 0.6 gather_fusion
  5.8 0.1 broadcast_select_fusion
  5.8 1.0 fusion.6
  6.8 0.7 concatenate.14
  7.6 0.7 compare_and_fusion.2
  8.3 0.6 gather_fusion.1
  8.8 0.1 broadcast_in_dim.91
  8.9 0.1 broadcast_in_dim.92
  9.0 0.1 broadcast_in_dim.94
  9.1 0.1 broadcast_in_dim.95
  9.2 0.3 fusion
  9.5 29.4 %shard_map.120 = f32[8,4,104,128]{3,2,1,0:T(8,128)S(1)} custom-call(f32[8,104,128]{2,1,0:T(8,128)S(1)} %bitcast.54), custom_call_target="tpu_custom_call" | custom-call | tf_op jit(solution)/shard_map/pallas_call | solution.py:267
  38.9 0.1 copy.64
  39.1 0.1 slice.55
  39.2 0.2 slice_bitcast_fusion.1
  39.4 0.1 copy.65
  39.4 0.1 copy.66
  39.5 1.2 copy.67
  40.7 2.7 %select_maximum_fusion.refs_2_ = f32[3,512,384]{2,1,0:T(8,128)} fusion(f32[3,512,2]{2,1,0:T(8,128)} %bitcast.63, f32[3,512,128]{2,1,0:T(8,128)S(1)} %bitcast.62, f32[3,512,128]{2,1,0:T(8,128)S(1)} %bitcast.61), kind=kLoop, calls=%fused_computation.4 | loop fusion | flops 2359296 | bytes 3944448 | tf_op jit(solution)/shard_map/concatenate | solution.py:332
  43.4 0.1 div.104
  43.5 0.1 broadcast_in_dim.108
  43.7 0.1 gather.18
  43.7 0.1 select_multiply_fusion
  43.8 0.1 broadcast_in_dim.107
  43.9 0.1 copy.70
  44.0 0.1 broadcast_bitcast_fusion.refs_3_
  44.1 0.1 pad.23.clone
  44.2 0.2 copy.57
  44.4 0.0 copy-start.1
  44.4 0.0 copy-start
  44.5 1.4 maximum_maximum_fusion.refs_0_
  45.9 0.1 copy.58
  46.1 109.7 %shard_map.121 = (f32[1024,384]{1,0:T(8,128)S(1)}, f32[256,384]{1,0:T(8,128)S(1)}) custom-call(f32[1024,384]{1,0:T(8,128)S(1)} %maximum_maximum_fusion.refs_0_, f32[256,384]{1,0:T(8,128)S(1)} %maximum_maximum_fusion.1.refs_1_, f32[3,512,384]{2,1,0:T(8,128)} %select_maximum_fusion.refs_2_, f32[3,8,512]{2,1,0:T(8,128)S(1)} %broadcast_bitcast_fusion.refs_3_, ...), custom_call_target="tpu_custom_call" | custom-call | tf_op jit(solution)/shard_map/pallas_call | solution.py:181
  155.8 1.1 slice.43
  156.9 0.7 slice.45
  157.6 0.8 negate_reduce_fusion
  158.4 0.7 slice_reduce_fusion
  (26 shorter events, 0.3 us)
Async XLA Ops:
  40.7 3.5 %copy-start.2 = (f32[1024]{0:T(1024)S(1)}, f32[1024]{0:T(1024)}, u32[]{:S(2)}) copy-start(f32[1024]{0:T(1024)} %param.12) | copy-start | bytes 12292
  44.4 1.4 copy-start.1
  44.4 1.6 copy-start

commit v3 on v2

--- a/solution.py
+++ b/solution.py
@@ -1,3 +1,5 @@
+import math
+
 import jax
 import jax.numpy as jnp
 from jax import lax
@@ -49,11 +51,13 @@
         parts = [panel[:, LANES * q : LANES * (q + 1)] for q in range(3)]
         root = roots[start : start + PANEL, :]
         for r in range(PANEL):
-            pivot = cols[r][r : r + 1, :]
+            mine = cols[r]
+            pivot = mine[r : r + 1, :]
             inv = lax.rsqrt(pivot)
-            column = cols[r] * inv
+            inv_pivot = inv * inv
             for t in range(r + 1, PANEL):
-                cols[t] = cols[t] - column * column[t : t + 1, :]
+                cols[t] = cols[t] - (mine * mine[t : t + 1, :]) * inv_pivot
+            column = mine * inv
             below = jnp.where(rows > r, column, 0.0)
             shifted = 1.0 / (pivot * inv + root[r : r + 1, :])
             for q, scale in enumerate((inv, inv, shifted)):
@@ -72,19 +76,21 @@
 
 
 def analysis_kernel(
-    members, state_in, obs_in, batch_in, tw_state, tw_obs, tw_batch, state, obs, batch, work, sgh, roots, inverses, y_hi, y_lo, z, z_hi, z_lo
+    members, state_in, mean_in, obs_in, depart_in, batch_in, tw_state, tw_obs, tw_batch, state, mean, obs, depart, batch, work, sgh, roots, inverses, y_hi, y_lo, z, z_hi, z_lo
 ):
     steps, size, width = batch_in.shape
     blocks = size // TAPER_BLOCK
     state[...] = state_in[...]
+    mean[...] = mean_in[...]
     obs[...] = obs_in[...]
+    depart[...] = depart_in[...]
+    state_rows = TAPER_BLOCK * math.gcd(state.shape[0] // TAPER_BLOCK, 4)
     for k in range(steps):
         batch[k] = batch_in[k]
     eye = (
         lax.broadcasted_iota(jnp.int32, (TAPER_BLOCK, LANES), 0)
         == lax.broadcasted_iota(jnp.int32, (TAPER_BLOCK, LANES), 1)
     ).astype(f32)
-    lane = lax.broadcasted_iota(jnp.int32, (TAPER_BLOCK, LANES), 1)
     extra = size + members
 
     def one_batch(k, carry):
@@ -112,65 +118,69 @@
             work[mine, size:extra] = dot(sgh[:, 2 * LANES :], work[mine, size:extra])
             work[mine, extra:] = dot(inverse, work[mine, extra:])
 
-            def trail(i, carry):
-                lower = pl.ds(pl.multiple_of(i * TAPER_BLOCK, TAPER_BLOCK), TAPER_BLOCK)
-                work[lower, :] = work[lower, :] - dot(work[mine, lower].T, work[mine, :])
-                return carry
-
-            return lax.fori_loop(j + 1, blocks, trail, carry)
+            for last in range(blocks - 1):
+                @pl.when(j == last)
+                def trail(edge=(last + 1) * TAPER_BLOCK):
+                    factor = work[mine, edge:size].T
+                    work[edge:, edge:] = work[edge:, edge:] - dot(factor, work[mine, edge:])
+
+            return carry
 
         lax.fori_loop(0, blocks, eliminate, 0)
 
-        def back(step, carry):
-            j = blocks - 1 - step
-            mine = pl.ds(pl.multiple_of(j * TAPER_BLOCK, TAPER_BLOCK), TAPER_BLOCK)
-
-            def gather(i, acc):
-                lower = pl.ds(pl.multiple_of(i * TAPER_BLOCK, TAPER_BLOCK), TAPER_BLOCK)
-                return acc - dot(work[mine, lower], z[lower, :])
-
-            acc = lax.fori_loop(j + 1, blocks, gather, work[mine, size:])
+        for j in reversed(range(blocks)):
+            mine, edge = slice(j * TAPER_BLOCK, (j + 1) * TAPER_BLOCK), (j + 1) * TAPER_BLOCK
+            acc = work[mine, size:]
+            if edge < size:
+                acc = acc - dot(work[mine, edge:size], z[edge:, :])
             z[mine, :] = dot(inverses[j].T, acc)
-            return carry
-
-        lax.fori_loop(0, blocks, back, 0)
         for j in range(blocks):
             mine = slice(j * TAPER_BLOCK, (j + 1) * TAPER_BLOCK)
-            tail = jnp.where(lane == 0, z[mine, members:], 0.0)
+            tail = jnp.broadcast_to(z[mine, members : members + 1], (TAPER_BLOCK, LANES))
             full = jnp.concatenate([z[mine, :members], tail], axis=1)
             hi, lo = split2(full)
             z_hi[mine, :] = hi
             z_lo[mine, :] = lo
 
-        def updated(x, weights):
-            covar = dot3(x[:, :members], y_hi[...], y_lo[...], ((1,), (1,))) * weights
-            return x - dot3(covar, z_hi[...], z_lo[...])
-
-        def state_block(i, carry):
-            mine = pl.ds(pl.multiple_of(i * TAPER_BLOCK, TAPER_BLOCK), TAPER_BLOCK)
-            state[mine, :] = updated(state[mine, :], tw_state[k, pl.ds(i, 1), :])
-            return carry
-
-        lax.fori_loop(0, state.shape[0] // TAPER_BLOCK, state_block, 0)
-        groups = tw_obs.shape[1]
-        high = obs.shape[0] // groups
+        def change(x, weights):
+            covar = dot3(x, y_hi[...], y_lo[...], ((1,), (1,)))
+            high = x.shape[0] // weights.shape[0]
+            parts = [covar[g * high : (g + 1) * high] * weights[g : g + 1, :] for g in range(weights.shape[0])]
+            covar = jnp.concatenate(parts, axis=0) if len(parts) > 1 else parts[0]
+            return dot3(covar, z_hi[...], z_lo[...])
+
+        def picked(delta, g, high):
+            tail = delta[g * high : (g + 1) * high, members : members + high]
+            return jnp.sum(tail * eye[:high, :high], axis=0, keepdims=True)
+
+        several = state_rows // TAPER_BLOCK
+        for first in range(0, tw_state.shape[1], several):
+            mine = slice(first * TAPER_BLOCK, first * TAPER_BLOCK + state_rows)
+            delta = change(state[mine, :], tw_state[k, first : first + several, :])
+            state[mine, :] = state[mine, :] - delta[:, :members]
+            for g in range(several):
+                one = slice(first + g, first + g + 1)
+                mean[one, :] = mean[one, :] + picked(delta, g, TAPER_BLOCK)
+        groups, high = depart.shape
+        delta = change(obs[...], tw_obs[k])
+        obs[...] = obs[...] - delta[:, :members]
         for g in range(groups):
-            mine = slice(g * high, (g + 1) * high)
-            obs[mine, :] = updated(obs[mine, :], tw_obs[k, g : g + 1, :])
-
-        def later(i, carry):
-            which = i // blocks
-            mine = pl.ds(pl.multiple_of(lax.rem(i, blocks) * TAPER_BLOCK, TAPER_BLOCK), TAPER_BLOCK)
-            batch[which, mine, :] = updated(batch[which, mine, :], tw_batch[k, pl.ds(i, 1), :])
-            return carry
-
-        lax.fori_loop((k + 1) * blocks, steps * blocks, later, 0)
+            depart[g : g + 1, :] = depart[g : g + 1, :] - picked(delta, g, high)
+
+        lane = lax.broadcasted_iota(jnp.int32, (size, LANES), 1)
+        for i in range(1, steps):
+            @pl.when(i > k)
+            def later(i=i):
+                delta = change(batch[i, :, :members], tw_batch[k, i * blocks : (i + 1) * blocks, :])
+                batch[i, :, :members] = batch[i, :, :members] - delta[:, :members]
+                batch[i, :, members:] = batch[i, :, members:] - jnp.where(lane == 0, delta[:, members:], 0.0)
+
         return carry
 
     lax.fori_loop(0, steps, one_batch, 0)
 
 
-def analyse(members, state, obs, batch, tw_state, tw_obs, tw_batch):
+def analyse(members, state, mean, obs, depart, batch, tw_state, tw_obs, tw_batch):
     steps, size, width = batch.shape
     blocks = size // TAPER_BLOCK
     vmem = pl.BlockSpec(memory_space=pltpu.VMEM)
@@ -180,9 +190,9 @@
 
     return pl.pallas_call(
         kernel,
-        out_shape=(jax.ShapeDtypeStruct(state.shape, f32), jax.ShapeDtypeStruct(obs.shape, f32)),
-        in_specs=[vmem] * 6,
-        out_specs=(vmem, vmem),
+        out_shape=tuple(jax.ShapeDtypeStruct(v.shape, f32) for v in (state, mean, obs, depart)),
+        in_specs=[vmem] * 8,
+        out_specs=(vmem,) * 4,
         scratch_shapes=[
             pltpu.VMEM(batch.shape, f32),
             pltpu.VMEM((size, size + width), f32),
@@ -196,7 +206,7 @@
             pltpu.VMEM((size, width), bf16),
         ],
         compiler_params=pltpu.CompilerParams(vmem_limit_bytes=48 * 1024 * 1024),
-    )(state, obs, batch, tw_state, tw_obs, tw_batch)
+    )(state, mean, obs, depart, batch, tw_state, tw_obs, tw_batch)
 
 
 def spread_kernel(mesh_axes, share, out, landed, *sems):
@@ -334,25 +344,18 @@
     between = small[:: TAPER_BLOCK // pieces, :, 2, : steps * blocks].transpose(1, 0, 2)
     tw_batch = columns(between.reshape(steps * blocks, steps, blocks)).transpose(1, 0, 2)
 
-    def widened(rows, column):
-        pad = jnp.zeros((rows.shape[0], LANES - 1), f32)
-        return jnp.concatenate([rows, column[:, None], pad], axis=1)
-
-    state, obs = analyse(
+    state, mean, obs, depart = analyse(
         members,
-        widened(state_anom, -state_mean),
-        widened(obs_anom.reshape(-1, members), obs_depart.reshape(-1)),
+        state_anom,
+        state_mean.reshape(-1, TAPER_BLOCK),
+        obs_anom.reshape(-1, members),
+        obs_depart.reshape(-1, high),
         batch,
         tw_state,
         tw_obs,
         tw_batch,
     )
-    return (
-        state[:, :members],
-        -state[:, members],
-        obs[:, :members].reshape(obs_anom.shape),
-        obs[:, members].reshape(obs_depart.shape),
-    )
+    return state, mean.reshape(-1), obs.reshape(obs_anom.shape), depart.reshape(obs_depart.shape)
 
 
 def solution(mesh):

time: 159 us -> 132 us (0.83)
  Pallas kernels: 139 us -> 119 us
  other arithmetic: 7.72 us -> 2.94 us
  local copies, waits for them, and re-layouts: 11.3 us -> 8.59 us
    pallas_call x1, Pallas kernels: 110 us -> 89.9 us  [analyse(): pl.pallas_call(kernel, out_shape=tuple((jax.ShapeDtypeStruct(v.shape, f32...]
    concatenate x1, other arithmetic: 2.71 us -> 0.2 us  [per_device(): jnp.concatenate(anomalies + [jnp.pad(columns_in, ((0, 0), (0, 0), (0, LAN...]
    slice x3 -> x0, local copies, waits for them, and re-layouts: 2.45 us -> none  [the longest x1 1.05 us: per_device(): state[:, :members]]
where the time goes in v3:
time: 132 us
  Pallas kernels  119 us (90%)
  local copies, waits for them, and re-layouts  8.59 us (7%)
  other arithmetic  2.94 us (2%)
    pallas_call x1, Pallas kernels, analyse(): pl.pallas_call(kernel, out_shape=tuple((jax.ShapeDtypeStruct(v.shape, f32...  89.9 us
    pallas_call x1, Pallas kernels, spread(): pl.pallas_call(kernel, out_shape=jax.ShapeDtypeStruct((regions, shards) +...  29.4 us

profile of v3, /device:TPU:0, one launch (start us, length us, event | category | flops | bytes accessed | tf_op | source)
XLA Modules:
  0.0 131.7 jit_solution(9065912093961025056)
XLA Ops:
  0.7 0.7 broadcast_multiply_fusion.1
  1.4 0.7 compare_and_fusion.2
  2.0 0.1 broadcast_in_dim.82
  2.1 0.1 broadcast_in_dim.83
  2.2 0.1 broadcast_in_dim.79
  2.3 0.1 broadcast_in_dim.80
  2.4 0.1 iota_add_fusion
  2.4 0.1 add.132
  2.6 0.8 copy.62
  3.3 0.6 gather_fusion.3
  3.9 0.8 copy.53
  4.7 0.6 gather_fusion.2
  5.2 0.1 select_bitcast_fusion.1
  5.3 0.1 copy.54
  5.4 0.1 copy.63
  5.5 0.7 select_reduce_fusion
  6.2 0.6 gather_fusion
  6.8 0.1 broadcast_select_fusion
  6.9 0.1 gather.18
  7.0 0.1 select_multiply_fusion
  7.0 0.1 copy.64
  7.1 0.1 broadcast_in_dim.95
  7.2 0.1 broadcast_bitcast_fusion.refs_5_
  7.3 1.0 fusion.6
  8.3 0.7 concatenate.6
  9.0 0.6 gather_fusion.1
  9.6 0.3 fusion
  9.9 29.4 %shard_map.120 = f32[8,4,104,128]{3,2,1,0:T(8,128)S(1)} custom-call(f32[8,104,128]{2,1,0:T(8,128)S(1)} %bitcast.53), custom_call_target="tpu_custom_call" | custom-call | tf_op jit(solution)/shard_map/pallas_call | solution.py:277
  39.4 0.1 copy.58
  39.5 0.1 slice.39
  39.7 0.2 slice_bitcast_fusion.1
  39.8 0.1 copy.59
  39.9 0.1 div.104
  40.0 0.1 broadcast_in_dim.96
  40.1 0.3 copy.61
  40.4 0.1 copy.60
  40.5 0.0 copy-start
  40.5 0.0 copy-start.1
  40.5 0.0 copy-start.2
  40.5 0.0 copy-start.3
  40.5 0.2 select_maximum_fusion.refs_4_
  40.7 0.7 copy-done
  41.4 0.4 copy-done.1
  41.8 0.0 copy-done.2
  41.8 0.0 copy-done.3
  41.8 89.9 %shard_map.121 = (f32[1024,256]{1,0:T(8,128)}, f32[8,128]{1,0:T(8,128)}, f32[256,256]{1,0:T(8,128)}, f32[2,128]{1,0:T(2,128)}) custom-call(f32[1024,256]{1,0:T(8,128)S(1)} %copy-done.1, f32[8,128]{1,0:T(8,128)S(1)} %bitcast.58, f32[256,256]{1,0:T(8,128)S(1)} %bitcast.54, f32[2,128]{1,0:T(2,128)S(1)} %copy-done.2, ...), custom_call_target="tpu_custom_call" | custom-call | tf_op jit(solution)/shard_map/pallas_call | solution.py:191
  (19 shorter events, 0.2 us)
Async XLA Ops:
  40.5 1.0 copy-start
  40.5 1.3 copy-start.1
  40.5 1.3 copy-start.2
  40.5 1.3 copy-start.3

commit v4 on v3

--- a/solution.py
+++ b/solution.py
@@ -10,6 +10,7 @@
 TAPER_BLOCK = 128
 LANES = 128
 PANEL = 16
+HALF = 8
 highest = lax.Precision.HIGHEST
 f32 = jnp.float32
 bf16 = jnp.bfloat16
@@ -41,28 +42,44 @@
 
 
 def factor_block(sgh, roots):
-    rows = lax.broadcasted_iota(jnp.int32, (PANEL, LANES), 0)
+    rows = lax.broadcasted_iota(jnp.int32, (HALF, LANES), 0)
+    halves = PANEL // HALF
     for start in range(0, TAPER_BLOCK, PANEL):
-        panel = sgh[start : start + PANEL, :]
+        panel = [sgh[start + HALF * h : start + HALF * (h + 1), :] for h in range(halves)]
         cols = [
-            jnp.broadcast_to(panel[:, start + t : start + t + 1], (PANEL, LANES))
+            [
+                jnp.broadcast_to(panel[h][:, start + t : start + t + 1], (HALF, LANES)) if h >= t // HALF else None
+                for h in range(halves)
+            ]
             for t in range(PANEL)
         ]
-        parts = [panel[:, LANES * q : LANES * (q + 1)] for q in range(3)]
-        root = roots[start : start + PANEL, :]
+        parts = [[panel[h][:, LANES * q : LANES * (q + 1)] for h in range(halves)] for q in range(3)]
+        root = [roots[start + HALF * h : start + HALF * (h + 1), :] for h in range(halves)]
         for r in range(PANEL):
-            mine = cols[r]
-            pivot = mine[r : r + 1, :]
+            mine, home, at = cols[r], r // HALF, slice(r % HALF, r % HALF + 1)
+            pivot = mine[home][at, :]
             inv = lax.rsqrt(pivot)
             inv_pivot = inv * inv
-            for t in range(r + 1, PANEL):
-                cols[t] = cols[t] - (mine * mine[t : t + 1, :]) * inv_pivot
-            column = mine * inv
-            below = jnp.where(rows > r, column, 0.0)
-            shifted = 1.0 / (pivot * inv + root[r : r + 1, :])
+            for h in range(home, halves):
+                scaled = mine[h] * inv_pivot
+                for t in range(r + 1, PANEL):
+                    if h >= t // HALF:
+                        row = mine[t // HALF][t % HALF : t % HALF + 1, :]
+                        if t == r + 1:
+                            cols[t][h] = cols[t][h] - (mine[h] * row) * inv_pivot
+                        else:
+                            cols[t][h] = cols[t][h] - scaled * row
+            shifted = 1.0 / (pivot * inv + root[home][at, :])
             for q, scale in enumerate((inv, inv, shifted)):
-                done = parts[q][r : r + 1, :] * scale
-                parts[q] = jnp.where(rows == r, done, parts[q] - below * done)
+                done = parts[q][home][at, :] * scale
+                for h in range(home, halves):
+                    column = mine[h] * inv
+                    if h == home:
+                        below = jnp.where(rows > r % HALF, column, 0.0)
+                        parts[q][h] = jnp.where(rows == r % HALF, done, parts[q][h] - below * done)
+                    else:
+                        parts[q][h] = parts[q][h] - column * done
+        parts = [jnp.concatenate(part, axis=0) for part in parts]
         solved = jnp.concatenate(parts, axis=1)
         sgh[start : start + PANEL, :] = solved
         after = start + PANEL
@@ -304,15 +321,16 @@
     def columns(weights):
         return jnp.repeat(weights, TAPER_BLOCK, axis=-1) / (members - 1)
 
-    wanted = (batch_order[:, None] * blocks + jnp.arange(blocks, dtype=jnp.int32)).reshape(-1)
-    state_weights = lookup(taper_levels, jnp.take(state_taper, wanted, axis=1))
-    tw_state = columns(state_weights.reshape(-1, steps, blocks)).transpose(1, 0, 2)
-    obs_weights = lookup(taper_levels, jnp.take(obs_taper, wanted, axis=1))
     high = min(pieces, TAPER_BLOCK)
     group_rows = jnp.arange(per_region * pieces // high, dtype=jnp.int32) * high
     group_block = (group_rows // pieces * size + shard * pieces + group_rows % pieces) // TAPER_BLOCK
-    mine = jnp.take(obs_weights, group_block, axis=0)
-    tw_obs = columns(mine.reshape(-1, steps, blocks)).transpose(1, 0, 2)
+    index = jnp.concatenate([state_taper, jnp.take(obs_taper, group_block, axis=0)], axis=0)
+    index = jnp.take(index.reshape(index.shape[0], -1, blocks), batch_order, axis=1)
+    weights = lookup(taper_levels, index)
+    spread_weights = columns(weights).transpose(1, 0, 2)
+    tw_state = spread_weights[:, : state_taper.shape[0]]
+    tw_obs = spread_weights[:, state_taper.shape[0] :]
+    mine = weights[state_taper.shape[0] :].reshape(-1, steps * blocks)
 
     regions, shards = lax.axis_size("region"), lax.axis_size("shard")
     halves = members // LANES

time: 132 us -> 130 us (0.985)
  local copies, waits for them, and re-layouts: 8.59 us -> 6.6 us
    unnamed x10, local copies, waits for them, and re-layouts: 2.63 us -> 1.13 us
where the time goes in v4:
time: 130 us; the launch traced here: 129 us
  Pallas kernels  118 us (91%)
  local copies, waits for them, and re-layouts  6.6 us (5%)
  other arithmetic  3.45 us (3%)
    pallas_call x1, Pallas kernels, analyse(): pl.pallas_call(kernel, out_shape=tuple((jax.ShapeDtypeStruct(v.shape, f32...  88.9 us
    pallas_call x1, Pallas kernels, spread(): pl.pallas_call(kernel, out_shape=jax.ShapeDtypeStruct((regions, shards) +...  29.4 us

profile of v4, /device:TPU:0, one launch (start us, length us, event | category | flops | bytes accessed | tf_op | source)
XLA Modules:
  0.0 129.3 jit_solution(12574493132524233641)
XLA Ops:
  0.6 0.0 copy-start
  0.7 0.7 compare_select_fusion.3
  1.4 0.7 fusion.5
  2.0 0.1 broadcast_in_dim.76
  2.1 0.1 broadcast_in_dim.77
  2.2 0.1 broadcast_in_dim.79
  2.3 0.1 broadcast_in_dim.80
  2.4 0.0 copy-done
  2.4 0.6 gather_fusion
  2.9 0.1 broadcast_select_fusion
  3.0 0.7 pad_add_fusion
  3.7 0.1 copy.58
  3.8 0.6 gather_fusion.1
  4.4 0.1 select_bitcast_fusion
  4.5 0.8 select_reduce_fusion
  5.2 0.1 slice.49
  5.3 0.1 copy.59
  5.4 0.1 reshape.216
  5.5 0.1 copy.67
  5.6 0.1 broadcast_in_dim.94
  5.8 1.0 fusion.6
  6.8 0.7 concatenate.10
  7.6 0.6 gather_fusion.2
  8.2 0.3 fusion
  8.5 29.4 %shard_map.120 = f32[8,4,104,128]{3,2,1,0:T(8,128)S(1)} custom-call(f32[8,104,128]{2,1,0:T(8,128)S(1)} %bitcast.46), custom_call_target="tpu_custom_call" | custom-call | tf_op jit(solution)/shard_map/pallas_call | solution.py:294
  37.9 0.1 copy.63
  38.0 0.1 slice.50
  38.2 0.2 slice_bitcast_fusion.1
  38.4 0.1 copy.64
  38.4 0.1 div.90
  38.5 0.1 broadcast_in_dim.95
  38.7 0.3 copy.66
  39.0 0.1 copy.65
  39.0 0.0 copy-start.1
  39.1 0.0 copy-start.2
  39.1 0.0 copy-start.3
  39.1 0.0 copy-start.4
  39.1 0.2 select_maximum_fusion.refs_4_
  39.3 0.7 copy-done.1
  40.0 0.4 copy-done.2
  40.4 0.0 copy-done.3
  40.4 0.0 copy-done.4
  40.4 88.9 %shard_map.121 = (f32[1024,256]{1,0:T(8,128)}, f32[8,128]{1,0:T(8,128)}, f32[256,256]{1,0:T(8,128)}, f32[2,128]{1,0:T(2,128)}) custom-call(f32[1024,256]{1,0:T(8,128)S(1)} %copy-done.2, f32[8,128]{1,0:T(8,128)S(1)} %bitcast.50, f32[256,256]{1,0:T(8,128)S(1)} %bitcast.47, f32[2,128]{1,0:T(2,128)S(1)} %copy-done.3, ...), custom_call_target="tpu_custom_call" | custom-call | tf_op jit(solution)/shard_map/pallas_call | solution.py:208
  (18 shorter events, 0.2 us)
Async XLA Ops:
  0.6 1.8 %copy-start = (s32[8,64]{1,0:T(8,128)S(1)}, s32[8,64]{1,0:T(8,128)}, u32[]{:S(2)}) copy-start(s32[8,64]{1,0:T(8,128)} %param.16) | copy-start | bytes 6148
  39.0 1.0 copy-start.1
  39.1 1.3 %copy-start.2 = (f32[1024,256]{1,0:T(8,128)S(1)}, f32[1024,256]{1,0:T(8,128)}, u32[]{:S(2)}) copy-start(f32[1024,256]{1,0:T(8,128)} %refs_0_.1) | copy-start | bytes 3145732
  39.1 1.3 %copy-start.3 = (f32[2,128]{1,0:T(2,128)S(1)}, f32[2,128]{1,0:T(2,128)}, u32[]{:S(2)}) copy-start(f32[2,128]{1,0:T(2,128)} %refs_3_.1) | copy-start | bytes 3076
  39.1 1.3 copy-start.4
